TPU v7x, 128 devices: a whole 4x4x4 slice. The times are simulated.
128 devices in a mesh: dp: 4 (over y), pipe: 4 (over z), expert: 8 (over x, core).
Axes of the slice: x: 4, y: 4, z: 4, core: 2. Of those that a mesh axis runs over, the one named last changes fastest.
Arguments:
- tokens: bfloat16 [4, 4096, 5120], P('pipe', ('dp', 'expert')), may hold values from -6 to 6
- cotangent: bfloat16 [4, 4096, 5120], P('pipe', ('dp', 'expert')), may hold values from -6 to 6
- gain: float32 [4, 5120], P('pipe'), may hold values from 0.1 to 1.9
- w_gate: bfloat16 [4, 8, 5120, 768], P('pipe', 'expert', 'dp'), may hold values from -0.078125 to 0.078125
- w_up: bfloat16 [4, 8, 5120, 768], P('pipe', 'expert', 'dp'), may hold values from -0.078125 to 0.078125
- w_down: bfloat16 [4, 8, 768, 5120], P('pipe', 'expert', None, 'dp'), may hold values from -0.21875 to 0.21875
- route: int32 [4, 4, 512, 1], P('pipe', None, ('dp', 'expert')), may hold values from 0 to 7; in each aligned block of 16 rows (0 to 15, 16 to 31, ..., all dimensions but the last counted through in order) at most 3 rows name the same one
Outputs:
- out_tokens: bfloat16 [4, 4096, 5120], P('pipe', ('dp', 'expert'))
- grad_tokens: bfloat16 [4, 4096, 5120], P('pipe', ('dp', 'expert'))
- grad_gain: float32 [4, 5120], P('pipe')
- grad_gate: bfloat16 [4, 8, 5120, 768], P('pipe', 'expert', 'dp')
- grad_up: bfloat16 [4, 8, 5120, 768], P('pipe', 'expert', 'dp')
- grad_down: bfloat16 [4, 8, 768, 5120], P('pipe', 'expert', None, 'dp')
Inputs may be any that keep to these rules, and one draw needn't show every extreme that they name: route[l, m, t, 0] is the expert of tile t at layer l for micro-batch m. Among the 16 tiles of one device for one layer and one micro-batch (aligned blocks), no expert is named more than 3 times; every expert is named somewhere.
All inputs are finite; a program needn't handle non-finite values.
Results may differ from a plain program's by a relative error of at most 0.034.
Values may be sent and summed in bfloat16 or wider, within the bound.
A program may use at most 128 MiB of HBM per device.

v0:
```python
import jax
import jax.numpy as jnp
from jax import lax
from jax.sharding import PartitionSpec as P

TILE = 8
PASSES = 2
epsilon = 1e-06


def shifted(block, axis, distance):
    devices = range(lax.axis_size(axis))
    route = [((i - distance) % len(devices), i) for i in devices]
    return lax.ppermute(block, axis, route)


def contract_last(former, latter):
    return lax.dot_general(
        former, latter, (((1,), (1,)), ((), ())), preferred_element_type=jnp.float32
    )


def contract_first(former, latter):
    return lax.dot_general(
        former, latter, (((0,), (0,)), ((), ())), preferred_element_type=jnp.float32
    )


def normalize(hidden, gain_row):
    widened = hidden.astype(jnp.float32)
    inverse = lax.rsqrt(jnp.mean(widened * widened, axis=-1, keepdims=True) + epsilon)
    scaled = widened * inverse
    return ((scaled * gain_row).astype(jnp.bfloat16), scaled, inverse)


def slot_matrix(route_now, expert_count, capacity):
    tile_count = route_now.shape[0]
    expert_ids = jnp.arange(expert_count, dtype=jnp.int32)
    member = (route_now[None, :] == expert_ids[:, None]).astype(jnp.int32)
    earlier = jnp.cumsum(member, axis=1) - member
    rank_ids = jnp.arange(capacity, dtype=jnp.int32)
    placed = member[:, None, :] * (earlier[:, None, :] == rank_ids[None, :, None]).astype(jnp.int32)
    return placed.reshape(expert_count * capacity, tile_count)


def into_slots(placed, rows, tile_rows, dp_count):
    width = rows.shape[-1]
    tile_blocks = rows.reshape(placed.shape[1], tile_rows, dp_count, width // dp_count)
    return jnp.einsum(
        "st,trqd->qsrd",
        placed.astype(jnp.bfloat16),
        tile_blocks,
        preferred_element_type=jnp.float32,
    ).astype(jnp.bfloat16)


def from_slots(placed, slot_rows):
    merged = jnp.einsum(
        "st,qsrd->trqd", placed.astype(jnp.bfloat16), slot_rows, preferred_element_type=jnp.float32
    ).astype(jnp.bfloat16)
    return merged.reshape(merged.shape[0] * merged.shape[1], -1)


def send_out(slot_rows):
    quarter = slot_rows.shape[-1]
    flat = slot_rows.reshape((-1,) + slot_rows.shape[2:])
    arrived = lax.all_to_all(flat, ("dp", "expert"), split_axis=0, concat_axis=0, tiled=True)
    return arrived.reshape(-1, quarter)


def send_back(part_rows, dp_count, tile_rows):
    quarter = part_rows.shape[-1]
    flat = part_rows.reshape(-1, tile_rows, quarter)
    returned = lax.all_to_all(flat, ("dp", "expert"), split_axis=0, concat_axis=0, tiled=True)
    return returned.reshape(dp_count, -1, tile_rows, quarter)


def widen_rounded(values):
    return lax.optimization_barrier(values.astype(jnp.bfloat16)).astype(jnp.float32)


def expert_forward(received, gate_weight, up_weight, down_weight):
    gate_terms = widen_rounded(jnp.dot(received, gate_weight, preferred_element_type=jnp.float32))
    up_terms = widen_rounded(jnp.dot(received, up_weight, preferred_element_type=jnp.float32))
    gate_pre, up_pre = (
        lax.psum(gate_terms.astype(jnp.bfloat16), "dp").astype(jnp.float32),
        lax.psum(up_terms.astype(jnp.bfloat16), "dp").astype(jnp.float32),
    )
    activated = (jax.nn.silu(gate_pre) * up_pre).astype(jnp.bfloat16)
    part_rows = jnp.dot(activated, down_weight, preferred_element_type=jnp.float32).astype(
        jnp.bfloat16
    )
    return (part_rows, (gate_pre, up_pre, activated))


def expert_backward(
    received, grad_recv, kept_state, gate_weight, up_weight, down_weight, grad_sums
):
    gate_pre, up_pre, activated = kept_state
    grad_terms = widen_rounded(contract_last(grad_recv, down_weight))
    grad_act = lax.psum(grad_terms.astype(jnp.bfloat16), "dp").astype(jnp.float32)
    sigmoid_gate = jax.nn.sigmoid(gate_pre)
    silu_gate = gate_pre * sigmoid_gate
    grad_gate_pre = (
        grad_act * up_pre * sigmoid_gate * (1.0 + gate_pre * (1.0 - sigmoid_gate))
    ).astype(jnp.bfloat16)
    grad_up_pre = (grad_act * silu_gate).astype(jnp.bfloat16)
    back_rows = (
        contract_last(grad_gate_pre, gate_weight) + contract_last(grad_up_pre, up_weight)
    ).astype(jnp.bfloat16)
    grad_gate = grad_sums[0] + contract_first(received, grad_gate_pre)
    grad_up = grad_sums[1] + contract_first(received, grad_up_pre)
    grad_down = grad_sums[2] + contract_first(activated, grad_recv)
    return (back_rows, (grad_gate, grad_up, grad_down))


def body(tokens, cotangent, gain, w_gate, w_up, w_down, route):
    pipe_count = lax.axis_size("pipe")
    dp_count = lax.axis_size("dp")
    expert_count = lax.axis_size("expert")
    section_index = lax.axis_index("pipe")
    gain_row = gain[0]
    gate_weight = w_gate[0, 0]
    up_weight = w_up[0, 0]
    down_weight = w_down[0, 0]
    route_table = route[0, :, :, 0]
    tile_count = route_table.shape[1]
    capacity = max(2, 3 * tile_count // (2 * expert_count))
    hidden = tokens[0]
    saved_ticks = []
    out_rows = hidden
    for pass_index in range(PASSES):
        micro_index = (section_index - pass_index + pipe_count) % pipe_count
        route_now = lax.dynamic_index_in_dim(route_table, micro_index, 0, keepdims=False)
        placed = slot_matrix(route_now, expert_count, capacity)
        normed, scaled, inverse = normalize(hidden, gain_row)
        received = send_out(into_slots(placed, normed, TILE, dp_count))
        part_rows, kept_state = expert_forward(received, gate_weight, up_weight, down_weight)
        ffn_rows = from_slots(placed, send_back(part_rows, dp_count, TILE))
        new_hidden = (hidden.astype(jnp.float32) + ffn_rows.astype(jnp.float32)).astype(
            jnp.bfloat16
        )
        saved_ticks.append((placed, scaled, inverse, received, kept_state))
        if pass_index + 1 < PASSES:
            hidden = shifted(new_hidden, "pipe", 1)
        else:
            out_rows = new_hidden
    grad_rows = cotangent[0]
    grad_sums = (
        jnp.zeros(gate_weight.shape, jnp.float32),
        jnp.zeros(up_weight.shape, jnp.float32),
        jnp.zeros(down_weight.shape, jnp.float32),
    )
    gain_sum = jnp.zeros(gain_row.shape, jnp.float32)
    entry_grad = grad_rows
    for pass_index in reversed(range(PASSES)):
        placed, scaled, inverse, received, kept_state = saved_ticks[pass_index]
        grad_recv = send_out(into_slots(placed, grad_rows, TILE, dp_count))
        back_rows, grad_sums = expert_backward(
            received, grad_recv, kept_state, gate_weight, up_weight, down_weight, grad_sums
        )
        grad_normed = from_slots(placed, send_back(back_rows, dp_count, TILE)).astype(jnp.float32)
        gain_sum = gain_sum + jnp.sum(grad_normed * scaled, axis=0)
        grad_scaled = grad_normed * gain_row
        grad_wide = inverse * (
            grad_scaled - scaled * jnp.mean(grad_scaled * scaled, axis=-1, keepdims=True)
        )
        grad_in = (grad_rows.astype(jnp.float32) + grad_wide).astype(jnp.bfloat16)
        if pass_index > 0:
            grad_rows = shifted(grad_in, "pipe", -1)
        else:
            entry_grad = grad_in
    gain_total = lax.psum(gain_sum, ("dp", "expert"))
    return (
        out_rows[None],
        entry_grad[None],
        gain_total[None],
        grad_sums[0].astype(jnp.bfloat16)[None, None],
        grad_sums[1].astype(jnp.bfloat16)[None, None],
        grad_sums[2].astype(jnp.bfloat16)[None, None],
    )


def solution(mesh):
    placed = (
        P("pipe", ("dp", "expert"), None),
        P("pipe", ("dp", "expert"), None),
        P("pipe", None),
        P("pipe", "expert", "dp", None),
        P("pipe", "expert", "dp", None),
        P("pipe", "expert", None, "dp"),
        P("pipe", None, ("dp", "expert"), None),
    )
    return jax.shard_map(
        body,
        mesh=mesh,
        in_specs=placed,
        out_specs=(
            P("pipe", ("dp", "expert"), None),
            P("pipe", ("dp", "expert"), None),
            P("pipe", None),
            P("pipe", "expert", "dp", None),
            P("pipe", "expert", "dp", None),
            P("pipe", "expert", None, "dp"),
        ),
        check_vma=False,
    )
```

profile of v0, /device:TPU:0, one launch (start us, length us, event | category | flops | bytes accessed | tf_op | source)
XLA Modules:
  0.0 713.0 jit_solution(6603323839218652019)
XLA Ops:
  13.2 34.5 %all_to_all.40 = bf16[96,8,1280]{2,1,0:T(8,128)(2,1)S(1)} all-to-all(bf16[96,8,1280]{2,1,0:T(8,128)(2,1)S(1)} %copy.49), channel_id=1, replica_groups=mesh['dp'=4,'pipe'=4,'expert'=8] {'dp','expert'}, dimensions={0} | all-to-all | bytes 3932160 | tf_op jit(solution)/shard_map/all_to_all | solution.py:67
  53.2 62.0 %all-reduce.10.cloned.1.call-done = (bf16[768,768]{1,0:T(8,128)(2,1)}, bf16[768,768]{1,0:T(8,128)(2,1)}) async-done(((bf16[768,768]{1,0:T(8,128)(2,1)}, bf16[768,768]{1,0:T(8,128)(2,1)}), (bf16[768,768]{1,0:T(8,128)(2,1)}, bf16[768,768]{1,0:T(8,128)(2,1)})) %all-reduce.10.cloned.1.call-update) | async-done | bytes 2359312 | tf_op jit(solution)/shard_map/psum | solution.py:87
  118.9 32.6 %all_to_all.41 = bf16[96,8,1280]{2,1,0:T(8,128)(2,1)S(1)} all-to-all(bf16[96,8,1280]{2,1,0:T(8,128)(2,1)S(1)} %fusion.12), channel_id=1, replica_groups=mesh['dp'=4,'pipe'=4,'expert'=8] {'dp','expert'}, dimensions={0} | all-to-all | bytes 3932160 | tf_op jit(solution)/shard_map/all_to_all | solution.py:74
  163.1 4.9 all-to-all-start.4
  167.9 20.4 %collective-permute-done = bf16[128,5120]{1,0:T(8,128)(2,1)} collective-permute-done((bf16[128,5120]{1,0:T(8,128)(2,1)}, bf16[128,5120]{1,0:T(8,128)(2,1)}, u32[]{:S(2)}, u32[]{:S(2)}) %collective-permute-start) | collective-permute-done | bytes 1310752 | tf_op jit(solution)/shard_map/ppermute | solution.py:14
  196.4 4.7 all-to-all-start.2
  201.2 4.3 fusion.114
  205.4 24.1 %all-to-all-done.2 = bf16[96,8,1280]{2,1,0:T(8,128)(2,1)} async-done(((bf16[96,8,1280]{2,1,0:T(8,128)(2,1)}), bf16[96,8,1280]{2,1,0:T(8,128)(2,1)}, u32[]{:S(2)}, u32[]{:S(2)}) %all-to-all-start.2) | async-done | bytes 1966112 | tf_op jit(solution)/shard_map/all_to_all | solution.py:67
  229.5 5.0 fusion.104
  234.5 4.3 fusion.109
  238.8 79.5 %all-reduce.8.cloned.1.call-done = (bf16[768,768]{1,0:T(8,128)(2,1)}, bf16[768,768]{1,0:T(8,128)(2,1)}, bf16[768,768]{1,0:T(8,128)(2,1)}) async-done(((bf16[768,768]{1,0:T(8,128)(2,1)}, bf16[768,768]{1,0:T(8,128)(2,1)}, bf16[768,768]{1,0:T(8,128)(2,1)}), (bf16[768,768]{1,0:T(8,128)(2,1)}, bf16[768,768]{1,0:T(8,128)(2,1)}, bf16[768,768]{1,0:T(8,128)(2,1)})) %all-reduce.8.cloned.1.call-update) | async-done | bytes 3538960 | tf_op jit(solution)/shard_map/psum | solution.py:87
  318.3 5.0 fusion.13
  323.4 5.9 all-to-all-start.3
  329.3 5.3 fusion.81
  338.1 19.6 %all-to-all-done.3 = bf16[96,8,1280]{2,1,0:T(8,128)(2,1)} async-done(((bf16[96,8,1280]{2,1,0:T(8,128)(2,1)}), bf16[96,8,1280]{2,1,0:T(8,128)(2,1)}, u32[]{:S(2)}, u32[]{:S(2)}) %all-to-all-start.3) | async-done | bytes 1966112 | tf_op jit(solution)/shard_map/all_to_all | solution.py:74
  357.7 4.7 all-to-all-start.5
  368.2 22.7 %all-to-all-done.5 = bf16[96,8,1280]{2,1,0:T(8,128)(2,1)} async-done(((bf16[96,8,1280]{2,1,0:T(8,128)(2,1)}), bf16[96,8,1280]{2,1,0:T(8,128)(2,1)}, u32[]{:S(2)}, u32[]{:S(2)}) %all-to-all-start.5) | async-done | bytes 1966112 | tf_op jit(solution)/shard_map/all_to_all | solution.py:74
  404.1 26.3 %collective-permute-done.1 = bf16[128,5120]{1,0:T(8,128)(2,1)} collective-permute-done((bf16[128,5120]{1,0:T(8,128)(2,1)S(1)}, bf16[128,5120]{1,0:T(8,128)(2,1)}, u32[]{:S(2)}, u32[]{:S(2)}) %collective-permute-start.1) | collective-permute-done | bytes 1310752 | tf_op jit(solution)/shard_map/ppermute | solution.py:14
  438.7 5.3 all-to-all-start.6
  448.3 5.9 fusion.62
  454.2 18.3 %all-to-all-done.6 = bf16[96,8,1280]{2,1,0:T(8,128)(2,1)} async-done(((bf16[96,8,1280]{2,1,0:T(8,128)(2,1)}), bf16[96,8,1280]{2,1,0:T(8,128)(2,1)}, u32[]{:S(2)}, u32[]{:S(2)}) %all-to-all-start.6) | async-done | bytes 1966112 | tf_op jit(solution)/shard_map/all_to_all | solution.py:67
  472.5 4.3 fusion.119
  476.8 6.1 fusion.58
  482.9 5.5 fusion.64
  488.4 33.1 %all-reduce.6.cloned.1.call-done = bf16[768,768]{1,0:T(8,128)(2,1)} async-done(((bf16[768,768]{1,0:T(8,128)(2,1)}), bf16[768,768]{1,0:T(8,128)(2,1)}) %all-reduce.6.cloned.1.call-update) | async-done | bytes 1179664 | tf_op jit(solution)/shard_map/psum | solution.py:101
  521.5 5.3 fusion.79
  530.4 6.8 all-to-all-start.7
  537.3 6.7 fusion.18
  550.5 15.1 %all-to-all-done.7 = bf16[96,8,1280]{2,1,0:T(8,128)(2,1)} async-done(((bf16[96,8,1280]{2,1,0:T(8,128)(2,1)}), bf16[96,8,1280]{2,1,0:T(8,128)(2,1)}, u32[]{:S(2)}, u32[]{:S(2)}) %all-to-all-start.7) | async-done | bytes 1966112 | tf_op jit(solution)/shard_map/all_to_all | solution.py:74
  565.6 5.9 multiply_reduce_fusion
  571.5 125.2 %psum.55 = f32[1,5120]{1,0:T(1,128)} all-reduce(f32[1,5120]{1,0:T(1,128)S(1)} %bitcast.217), channel_id=1, replica_groups=mesh['dp'=4,'pipe'=4,'expert'=8] {'dp','expert'}, use_global_device_ids=true, to_apply=%region_14.15 | all-reduce | flops 5120 | bytes 40960 | tf_op jit(solution)/shard_map/psum | solution.py:173
  702.3 4.0 fusion.124
  (115 shorter events, 85.3 us)
Async XLA Ops:
  7.2 108.0 %copy-start = (bf16[1,1,768,1280]{3,2,1,0:T(8,128)(2,1)S(1)}, bf16[1,1,768,1280]{3,2,1,0:T(8,128)(2,1)}, u32[]{:S(2)}) copy-start(bf16[1,1,768,1280]{3,2,1,0:T(8,128)(2,1)} %param.12) | copy-start | bytes 5898244
  7.2 2.8 copy-start.1
  7.2 108.0 %all-reduce.10.cloned.1.call-start = ((), (), s32[]{:S(2)}) async-start(), calls=%async_computation.10 | async-start | bytes 4718592 | tf_op jit(solution)/shard_map/psum | solution.py:87
  13.2 34.5 %copy-start.7 = (bf16[1,1,1280,768]{3,2,1,0:T(8,128)(2,1)S(1)}, bf16[1,1,1280,768]{3,2,1,0:T(8,128)(2,1)}, u32[]{:S(2)}) copy-start(bf16[1,1,1280,768]{3,2,1,0:T(8,128)(2,1)} %param.10) | copy-start | bytes 5898244
  47.7 2.7 copy-start.8
  155.6 32.8 %collective-permute-start = (bf16[128,5120]{1,0:T(8,128)(2,1)}, bf16[128,5120]{1,0:T(8,128)(2,1)}, u32[]{:S(2)}, u32[]{:S(2)}) collective-permute-start(bf16[128,5120]{1,0:T(8,128)(2,1)} %fusion.29), channel_id=1, source_target_pairs={{24,0},{0,8},{8,16},{16,24},{25,1},{1,9},{9,17},{17,25},{26,2},{2,... | collective-permute-start | bytes 3932168 | tf_op jit(solution)/shard_map/ppermute | solution.py:14
  163.1 27.0 %copy-start.6 = (f32[1,5120]{1,0:T(1,128)S(1)}, f32[1,5120]{1,0:T(1,128)}, u32[]{:S(2)}) copy-start(f32[1,5120]{1,0:T(1,128)} %param.9) | copy-start | bytes 61444
  163.1 33.3 %all-to-all-start.4 = ((bf16[96,8,1280]{2,1,0:T(8,128)(2,1)}), bf16[96,8,1280]{2,1,0:T(8,128)(2,1)}, u32[]{:S(2)}, u32[]{:S(2)}) async-start(bf16[96,8,1280]{2,1,0:T(8,128)(2,1)} %copy.61), calls=%async_computation.4 | async-start | bytes 3932160 | tf_op jit(solution)/shard_map/all_to_all | solution.py:67
  196.4 33.2 %all-to-all-start.2 = ((bf16[96,8,1280]{2,1,0:T(8,128)(2,1)}), bf16[96,8,1280]{2,1,0:T(8,128)(2,1)}, u32[]{:S(2)}, u32[]{:S(2)}) async-start(bf16[96,8,1280]{2,1,0:T(8,128)(2,1)} %copy.55), calls=%async_computation.2 | async-start | bytes 3932160 | tf_op jit(solution)/shard_map/all_to_all | solution.py:67
  201.1 117.2 %all-reduce.8.cloned.1.call-start = ((), (), s32[]{:S(2)}) async-start(), calls=%async_computation.9 | async-start | bytes 7077888 | tf_op jit(solution)/shard_map/psum | solution.py:87
  229.5 5.0 copy-start.9
  323.4 34.3 %all-to-all-start.3 = ((bf16[96,8,1280]{2,1,0:T(8,128)(2,1)}), bf16[96,8,1280]{2,1,0:T(8,128)(2,1)}, u32[]{:S(2)}, u32[]{:S(2)}) async-start(bf16[96,8,1280]{2,1,0:T(8,128)(2,1)} %fusion.13), calls=%async_computation.3 | async-start | bytes 3932160 | tf_op jit(solution)/shard_map/all_to_all | solution.py:74
  329.3 5.3 copy-start.10
  329.3 5.3 copy-start.16
  329.3 5.3 copy-start.18
  357.7 33.2 %all-to-all-start.5 = ((bf16[96,8,1280]{2,1,0:T(8,128)(2,1)}), bf16[96,8,1280]{2,1,0:T(8,128)(2,1)}, u32[]{:S(2)}, u32[]{:S(2)}) async-start(bf16[96,8,1280]{2,1,0:T(8,128)(2,1)} %fusion.14), calls=%async_computation.5 | async-start | bytes 3932160 | tf_op jit(solution)/shard_map/all_to_all | solution.py:74
  401.2 29.2 %collective-permute-start.1 = (bf16[128,5120]{1,0:T(8,128)(2,1)S(1)}, bf16[128,5120]{1,0:T(8,128)(2,1)}, u32[]{:S(2)}, u32[]{:S(2)}) collective-permute-start(bf16[128,5120]{1,0:T(8,128)(2,1)S(1)} %get-tuple-element.15), channel_id=1, source_target_pairs={{8,0},{16,8},{24,16},{0,24},{9,1},{17,9},{25,17},{1,25},{10,2},{18... | collective-permute-start | bytes 3932168 | tf_op jit(solution)/shard_map/ppermute | solution.py:14
  438.7 33.7 %all-to-all-start.6 = ((bf16[96,8,1280]{2,1,0:T(8,128)(2,1)}), bf16[96,8,1280]{2,1,0:T(8,128)(2,1)}, u32[]{:S(2)}, u32[]{:S(2)}) async-start(bf16[96,8,1280]{2,1,0:T(8,128)(2,1)} %copy.67), calls=%async_computation.6 | async-start | bytes 3932160 | tf_op jit(solution)/shard_map/all_to_all | solution.py:67
  444.0 77.5 %all-reduce.6.cloned.1.call-start = ((), (), s32[]{:S(2)}) async-start(), calls=%async_computation.8 | async-start | bytes 2359296 | tf_op jit(solution)/shard_map/psum | solution.py:101
  476.8 6.2 copy-start.15
  476.8 6.1 copy-start.17
  476.8 6.1 copy-start.19
  521.5 5.3 copy-start.11
  521.5 5.3 copy-start.13
  521.5 5.3 copy-start.20
  530.4 35.3 %all-to-all-start.7 = ((bf16[96,8,1280]{2,1,0:T(8,128)(2,1)}), bf16[96,8,1280]{2,1,0:T(8,128)(2,1)}, u32[]{:S(2)}, u32[]{:S(2)}) async-start(bf16[96,8,1280]{2,1,0:T(8,128)(2,1)} %fusion.15), calls=%async_computation.7 | async-start | bytes 3932160 | tf_op jit(solution)/shard_map/all_to_all | solution.py:74
  537.2 6.8 copy-start.5
  537.2 6.8 copy-start.14
  537.2 6.8 copy-start.21
  537.2 6.8 copy-start.22
  544.0 3.2 copy-start.12
  544.0 3.2 copy-start.23
  (3 other events, 7.7 us)
Sparse Core Ops, SparseCore 0:
  53.3 61.8 all-reduce.9
  238.9 79.3 all-reduce.7
  476.9 44.5 all-reduce.5
where the time goes:
time: 723 us; the launch traced here: 713 us
  waiting for transfers between devices  322 us (45%)
  blocking collectives  192 us (27%)
  matrix products  98 us (14%)
  starting transfers between devices  37.9 us (5%)
  local copies, waits for them, and re-layouts  29.4 us (4%)
  other arithmetic  18.6 us (3%)
  between operations  14.4 us (2%)
    psum x2, waiting for transfers between devices, expert_forward(): lax.psum(up_terms.astype(jnp.bfloat16), 'dp').astype(jnp.float32)  142 us
    psum x1, blocking collectives, body(): gain_total = lax.psum(gain_sum, ('dp', 'expert'))  125 us
    all_to_all x3, waiting for transfers between devices, send_back(): lax.all_to_all(flat, ('dp', 'expert'), split_axis=0, concat_axis=0, tiled...  57.4 us
    ppermute x2, waiting for transfers between devices, shifted(): return lax.ppermute(block, axis, route)  46.7 us
    all_to_all x3, waiting for transfers between devices, send_out(): lax.all_to_all(flat, ('dp', 'expert'), split_axis=0, concat_axis=0, tiled...  43.6 us
    all_to_all x1, blocking collectives, send_out(): lax.all_to_all(flat, ('dp', 'expert'), split_axis=0, concat_axis=0, tiled...  34.5 us
    psum x1, waiting for transfers between devices, expert_backward(): lax.psum(grad_terms.astype(jnp.bfloat16), 'dp').astype(jnp.float32)  33.1 us
    all_to_all x1, blocking collectives, send_back(): lax.all_to_all(flat, ('dp', 'expert'), split_axis=0, concat_axis=0, tiled...  32.6 us
  transfers between devices with their start and end apart: 11, of which 11 were waited for; matrix products, arithmetic and copies ran while one was open for 9% of the time, Pallas kernels for 0%

commit v1 on v0

--- a/solution.py
+++ b/solution.py
@@ -1,3 +1,4 @@
+import functools
 import jax
 import jax.numpy as jnp
 from jax import lax
@@ -6,6 +7,13 @@
 TILE = 8
 PASSES = 2
 epsilon = 1e-06
+
+
+def knots_time(panel, dev_axis):
+    return jnp.sum(lax.all_gather(panel, dev_axis), 0)
+
+
+grid_close = functools.partial(knots_time, dev_axis="dp")
 
 
 def shifted(block, axis, distance):
@@ -98,7 +106,7 @@
 ):
     gate_pre, up_pre, activated = kept_state
     grad_terms = widen_rounded(contract_last(grad_recv, down_weight))
-    grad_act = lax.psum(grad_terms.astype(jnp.bfloat16), "dp").astype(jnp.float32)
+    grad_act = grid_close(grad_terms.astype(jnp.bfloat16)).astype(jnp.float32)
     sigmoid_gate = jax.nn.sigmoid(gate_pre)
     silu_gate = gate_pre * sigmoid_gate
     grad_gate_pre = (

time: 723 us -> 781 us (1.080)
  blocking collectives: 192 us -> 224 us
  waiting for transfers between devices: 322 us -> 336 us
  other arithmetic: 18.6 us -> 26.8 us
    all_gather x0 -> x2, waiting for transfers between devices: none -> 93.5 us  [knots_time(): return jnp.sum(lax.all_gather(panel, dev_axis), 0)]
    psum x2, waiting for transfers between devices: 142 us -> 106 us  [expert_forward(): lax.psum(up_terms.astype(jnp.bfloat16), 'dp').astype(jnp.float32)]
    psum x1 -> x0, waiting for transfers between devices: 33.1 us -> none  [expert_backward(): lax.psum(grad_terms.astype(jnp.bfloat16), 'dp').astype(jnp.float32)]
    all_to_all x1 -> x2, blocking collectives: 34.5 us -> 66.4 us  [send_out(): lax.all_to_all(flat, ('dp', 'expert'), split_axis=0, concat_axis=0, tiled...]
    all_to_all x3, waiting for transfers between devices: 57.4 us -> 37.4 us  [send_back(): lax.all_to_all(flat, ('dp', 'expert'), split_axis=0, concat_axis=0, tiled...]
    ppermute x2, starting transfers between devices: 4.94 us -> 16.9 us  [shifted(): return lax.ppermute(block, axis, route)]
    ppermute x2, waiting for transfers between devices: 46.7 us -> 56.9 us  [shifted(): return lax.ppermute(block, axis, route)]
    reduce_sum x0 -> x2, other arithmetic: none -> 8.13 us  [knots_time(): return jnp.sum(lax.all_gather(panel, dev_axis), 0)]
  transfers between devices with their start and end apart: 11 -> 11, of which waited for: 11 -> 10; matrix products, arithmetic and copies ran while one was open for 9% -> 10% of each run, Pallas kernels for 0% -> 0%
where the time goes in v1:
time: 781 us; the launch traced here: 771 us
  waiting for transfers between devices  336 us (43%)
  blocking collectives  224 us (29%)
  matrix products  95.4 us (12%)
  starting transfers between devices  44.7 us (6%)
  local copies, waits for them, and re-layouts  29.6 us (4%)
  other arithmetic  26.8 us (3%)
  between operations  14.5 us (2%)
    psum x1, blocking collectives, body(): gain_total = lax.psum(gain_sum, ('dp', 'expert'))  125 us
    psum x2, waiting for transfers between devices, expert_forward(): lax.psum(up_terms.astype(jnp.bfloat16), 'dp').astype(jnp.float32)  106 us
    all_gather x2, waiting for transfers between devices, knots_time(): return jnp.sum(lax.all_gather(panel, dev_axis), 0)  93.5 us
    all_to_all x2, blocking collectives, send_out(): lax.all_to_all(flat, ('dp', 'expert'), split_axis=0, concat_axis=0, tiled...  66.4 us
    ppermute x2, waiting for transfers between devices, shifted(): return lax.ppermute(block, axis, route)  56.9 us
    all_to_all x2, waiting for transfers between devices, send_out(): lax.all_to_all(flat, ('dp', 'expert'), split_axis=0, concat_axis=0, tiled...  42.3 us
    all_to_all x3, waiting for transfers between devices, send_back(): lax.all_to_all(flat, ('dp', 'expert'), split_axis=0, concat_axis=0, tiled...  37.4 us
    all_to_all x1, blocking collectives, send_back(): lax.all_to_all(flat, ('dp', 'expert'), split_axis=0, concat_axis=0, tiled...  32.6 us
  transfers between devices with their start and end apart: 11, of which 10 were waited for; matrix products, arithmetic and copies ran while one was open for 10% of the time, Pallas kernels for 0%

profile of v1, /device:TPU:0, one launch (start us, length us, event | category | flops | bytes accessed | tf_op | source)
XLA Modules:
  0.0 771.0 jit_solution(14418199186892424675)
XLA Ops:
  13.2 34.5 %all_to_all.40 = bf16[96,8,1280]{2,1,0:T(8,128)(2,1)S(1)} all-to-all(bf16[96,8,1280]{2,1,0:T(8,128)(2,1)S(1)} %copy.49), channel_id=1, replica_groups=mesh['dp'=4,'pipe'=4,'expert'=8] {'dp','expert'}, dimensions={0} | all-to-all | bytes 3932160 | tf_op jit(solution)/shard_map/all_to_all | solution.py:75
  53.2 62.0 %all-reduce.7.cloned.1.call-done = (bf16[768,768]{1,0:T(8,128)(2,1)}, bf16[768,768]{1,0:T(8,128)(2,1)}) async-done(((bf16[768,768]{1,0:T(8,128)(2,1)}, bf16[768,768]{1,0:T(8,128)(2,1)}), (bf16[768,768]{1,0:T(8,128)(2,1)}, bf16[768,768]{1,0:T(8,128)(2,1)})) %all-reduce.7.cloned.1.call-update) | async-done | bytes 2359312 | tf_op jit(solution)/shard_map/psum | solution.py:95
  118.9 32.6 %all_to_all.41 = bf16[96,8,1280]{2,1,0:T(8,128)(2,1)S(1)} all-to-all(bf16[96,8,1280]{2,1,0:T(8,128)(2,1)S(1)} %fusion.12), channel_id=1, replica_groups=mesh['dp'=4,'pipe'=4,'expert'=8] {'dp','expert'}, dimensions={0} | all-to-all | bytes 3932160 | tf_op jit(solution)/shard_map/all_to_all | solution.py:82
  155.6 13.9 %collective-permute-start = (bf16[128,5120]{1,0:T(8,128)(2,1)}, bf16[128,5120]{1,0:T(8,128)(2,1)}, u32[]{:S(2)}, u32[]{:S(2)}) collective-permute-start(bf16[128,5120]{1,0:T(8,128)(2,1)} %fusion.29), channel_id=1, source_target_pairs={{24,0},{0,8},{8,16},{16,24},{25,1},{1,9},{9,17},{17,25},{26,2},{2,... | collective-permute-start | bytes 3932168 | tf_op jit(solution)/shard_map/ppermute | solution.py:22
  169.7 30.6 %collective-permute-done = bf16[128,5120]{1,0:T(8,128)(2,1)} collective-permute-done((bf16[128,5120]{1,0:T(8,128)(2,1)}, bf16[128,5120]{1,0:T(8,128)(2,1)}, u32[]{:S(2)}, u32[]{:S(2)}) %collective-permute-start) | collective-permute-done | bytes 1310752 | tf_op jit(solution)/shard_map/ppermute | solution.py:22
  207.0 4.7 all-to-all-start.2
  217.0 23.1 %all-to-all-done.2 = bf16[96,8,1280]{2,1,0:T(8,128)(2,1)} async-done(((bf16[96,8,1280]{2,1,0:T(8,128)(2,1)}), bf16[96,8,1280]{2,1,0:T(8,128)(2,1)}, u32[]{:S(2)}, u32[]{:S(2)}) %all-to-all-start.2) | async-done | bytes 1966112 | tf_op jit(solution)/shard_map/all_to_all | solution.py:75
  240.2 4.7 all-to-all-start.4
  245.0 5.0 fusion.104
  250.0 4.3 fusion.109
  254.3 19.2 %all-to-all-done.4 = bf16[96,8,1280]{2,1,0:T(8,128)(2,1)} async-done(((bf16[96,8,1280]{2,1,0:T(8,128)(2,1)}), bf16[96,8,1280]{2,1,0:T(8,128)(2,1)}, u32[]{:S(2)}, u32[]{:S(2)}) %all-to-all-start.4) | async-done | bytes 1966112 | tf_op jit(solution)/shard_map/all_to_all | solution.py:75
  273.5 4.3 fusion.114
  277.8 43.5 %all-reduce.5.cloned.1.call-done = (bf16[768,768]{1,0:T(8,128)(2,1)}, bf16[768,768]{1,0:T(8,128)(2,1)}) async-done(((bf16[768,768]{1,0:T(8,128)(2,1)}, bf16[768,768]{1,0:T(8,128)(2,1)}), (bf16[768,768]{1,0:T(8,128)(2,1)}, bf16[768,768]{1,0:T(8,128)(2,1)})) %all-reduce.5.cloned.1.call-update) | async-done | bytes 2359312 | tf_op jit(solution)/shard_map/psum | solution.py:95
  321.3 5.0 fusion.13
  326.4 5.7 all-to-all-start.3
  332.1 63.4 %all-gather.5.cloned.1.call-done = bf16[3072,768]{1,0:T(8,128)(2,1)} async-done(((bf16[768,768]{1,0:T(8,128)(2,1)}), bf16[3072,768]{1,0:T(8,128)(2,1)}) %all-gather.5.cloned.1.call-update) | async-done | bytes 4718608 | tf_op jit(solution)/shard_map/all_gather | solution.py:13
  395.5 4.4 reduce_sum.82
  399.9 5.3 fusion.81
  408.7 5.6 all-to-all-start.5
  420.5 22.2 %all-to-all-done.5 = bf16[96,8,1280]{2,1,0:T(8,128)(2,1)} async-done(((bf16[96,8,1280]{2,1,0:T(8,128)(2,1)}), bf16[96,8,1280]{2,1,0:T(8,128)(2,1)}, u32[]{:S(2)}, u32[]{:S(2)}) %all-to-all-start.5) | async-done | bytes 1966112 | tf_op jit(solution)/shard_map/all_to_all | solution.py:82
  456.0 26.4 %collective-permute-done.1 = bf16[128,5120]{1,0:T(8,128)(2,1)} collective-permute-done((bf16[128,5120]{1,0:T(8,128)(2,1)S(1)}, bf16[128,5120]{1,0:T(8,128)(2,1)}, u32[]{:S(2)}, u32[]{:S(2)}) %collective-permute-start.1) | collective-permute-done | bytes 1310752 | tf_op jit(solution)/shard_map/ppermute | solution.py:22
  489.4 31.9 %all_to_all.42 = bf16[96,8,1280]{2,1,0:T(8,128)(2,1)S(1)} all-to-all(bf16[96,8,1280]{2,1,0:T(8,128)(2,1)S(1)} %copy.67), channel_id=1, replica_groups=mesh['dp'=4,'pipe'=4,'expert'=8] {'dp','expert'}, dimensions={0} | all-to-all | bytes 3932160 | tf_op jit(solution)/shard_map/all_to_all | solution.py:75
  529.3 6.2 fusion.58
  535.5 5.6 fusion.62
  541.1 5.4 fusion.64
  546.6 30.1 %all-gather.7.cloned.1.call-done = bf16[3072,768]{1,0:T(8,128)(2,1)} async-done(((bf16[768,768]{1,0:T(8,128)(2,1)}), bf16[3072,768]{1,0:T(8,128)(2,1)}) %all-gather.7.cloned.1.call-update) | async-done | bytes 4718608 | tf_op jit(solution)/shard_map/all_gather | solution.py:13
  580.4 5.2 fusion.79
  589.2 6.4 all-to-all-start.7
  595.7 6.7 fusion.18
  608.9 15.2 %all-to-all-done.7 = bf16[96,8,1280]{2,1,0:T(8,128)(2,1)S(1)} async-done(((bf16[96,8,1280]{2,1,0:T(8,128)(2,1)}), bf16[96,8,1280]{2,1,0:T(8,128)(2,1)S(1)}, u32[]{:S(2)}, u32[]{:S(2)}) %all-to-all-start.7) | async-done | bytes 1966112 | tf_op jit(solution)/shard_map/all_to_all | solution.py:82
  624.1 5.2 multiply_reduce_fusion
  629.3 125.2 %psum.39 = f32[1,5120]{1,0:T(1,128)} all-reduce(f32[1,5120]{1,0:T(1,128)S(1)} %bitcast.222), channel_id=1, replica_groups=mesh['dp'=4,'pipe'=4,'expert'=8] {'dp','expert'}, use_global_device_ids=true, to_apply=%region_14.15 | all-reduce | flops 5120 | bytes 40960 | tf_op jit(solution)/shard_map/psum | solution.py:181
  (123 shorter events, 92.8 us)
Async XLA Ops:
  7.2 108.0 %copy-start = (bf16[1,1,768,1280]{3,2,1,0:T(8,128)(2,1)S(1)}, bf16[1,1,768,1280]{3,2,1,0:T(8,128)(2,1)}, u32[]{:S(2)}) copy-start(bf16[1,1,768,1280]{3,2,1,0:T(8,128)(2,1)} %param.12) | copy-start | bytes 5898244
  7.2 2.8 copy-start.2
  7.2 108.0 %all-reduce.7.cloned.1.call-start = ((), (), s32[]{:S(2)}) async-start(), calls=%async_computation.11 | async-start | bytes 4718592 | tf_op jit(solution)/shard_map/psum | solution.py:95
  13.2 34.5 %copy-start.13 = (bf16[1,1,1280,768]{3,2,1,0:T(8,128)(2,1)S(1)}, bf16[1,1,1280,768]{3,2,1,0:T(8,128)(2,1)}, u32[]{:S(2)}) copy-start(bf16[1,1,1280,768]{3,2,1,0:T(8,128)(2,1)} %param.10) | copy-start | bytes 5898244
  154.2 47.7 %copy-start.12 = (f32[1,5120]{1,0:T(1,128)S(1)}, f32[1,5120]{1,0:T(1,128)}, u32[]{:S(2)}) copy-start(f32[1,5120]{1,0:T(1,128)} %param.9) | copy-start | bytes 61444
  155.6 44.7 %collective-permute-start = (bf16[128,5120]{1,0:T(8,128)(2,1)}, bf16[128,5120]{1,0:T(8,128)(2,1)}, u32[]{:S(2)}, u32[]{:S(2)}) collective-permute-start(bf16[128,5120]{1,0:T(8,128)(2,1)} %fusion.29), channel_id=1, source_target_pairs={{24,0},{0,8},{8,16},{16,24},{25,1},{1,9},{9,17},{17,25},{26,2},{2,... | collective-permute-start | bytes 3932168 | tf_op jit(solution)/shard_map/ppermute | solution.py:22
  207.0 33.2 %all-to-all-start.2 = ((bf16[96,8,1280]{2,1,0:T(8,128)(2,1)}), bf16[96,8,1280]{2,1,0:T(8,128)(2,1)}, u32[]{:S(2)}, u32[]{:S(2)}) async-start(bf16[96,8,1280]{2,1,0:T(8,128)(2,1)} %copy.55), calls=%async_computation.2 | async-start | bytes 3932160 | tf_op jit(solution)/shard_map/all_to_all | solution.py:75
  240.2 33.3 %all-to-all-start.4 = ((bf16[96,8,1280]{2,1,0:T(8,128)(2,1)}), bf16[96,8,1280]{2,1,0:T(8,128)(2,1)}, u32[]{:S(2)}, u32[]{:S(2)}) async-start(bf16[96,8,1280]{2,1,0:T(8,128)(2,1)} %copy.61), calls=%async_computation.4 | async-start | bytes 3932160 | tf_op jit(solution)/shard_map/all_to_all | solution.py:75
  244.9 76.4 %all-reduce.5.cloned.1.call-start = ((), (), s32[]{:S(2)}) async-start(), calls=%async_computation.10 | async-start | bytes 4718592 | tf_op jit(solution)/shard_map/psum | solution.py:95
  245.0 5.0 copy-start.15
  254.2 141.3 %all-gather.5.cloned.1.call-start = ((), (), s32[]{:S(2)}) async-start(), calls=%async_computation.8 | async-start | bytes 5898240 | tf_op jit(solution)/shard_map/all_gather | solution.py:13
  326.4 82.3 %all-to-all-start.3 = ((bf16[96,8,1280]{2,1,0:T(8,128)(2,1)}), bf16[96,8,1280]{2,1,0:T(8,128)(2,1)}, u32[]{:S(2)}, u32[]{:S(2)}) async-start(bf16[96,8,1280]{2,1,0:T(8,128)(2,1)} %fusion.13), calls=%async_computation.3 | async-start | bytes 3932160 | tf_op jit(solution)/shard_map/all_to_all | solution.py:82
  399.9 5.3 copy-start.8
  399.9 5.3 copy-start.16
  399.9 5.3 copy-start.22
  408.7 34.1 %all-to-all-start.5 = ((bf16[96,8,1280]{2,1,0:T(8,128)(2,1)}), bf16[96,8,1280]{2,1,0:T(8,128)(2,1)}, u32[]{:S(2)}, u32[]{:S(2)}) async-start(bf16[96,8,1280]{2,1,0:T(8,128)(2,1)} %fusion.14), calls=%async_computation.5 | async-start | bytes 3932160 | tf_op jit(solution)/shard_map/all_to_all | solution.py:82
  414.3 162.3 %all-gather.7.cloned.1.call-start = ((), (), s32[]{:S(2)}) async-start(), calls=%async_computation.9 | async-start | bytes 5898240 | tf_op jit(solution)/shard_map/all_gather | solution.py:13
  453.1 29.3 %collective-permute-start.1 = (bf16[128,5120]{1,0:T(8,128)(2,1)S(1)}, bf16[128,5120]{1,0:T(8,128)(2,1)}, u32[]{:S(2)}, u32[]{:S(2)}) collective-permute-start(bf16[128,5120]{1,0:T(8,128)(2,1)S(1)} %get-tuple-element.14), channel_id=1, source_target_pairs={{8,0},{16,8},{24,16},{0,24},{9,1},{17,9},{25,17},{1,25},{10,2},{18... | collective-permute-start | bytes 3932168 | tf_op jit(solution)/shard_map/ppermute | solution.py:22
  529.3 6.2 copy-start.9
  529.3 6.2 copy-start.23
  535.5 5.6 copy-start.21
  580.4 5.3 copy-start.10
  580.4 5.3 copy-start.17
  580.4 5.3 copy-start.19
  589.2 34.9 %all-to-all-start.7 = ((bf16[96,8,1280]{2,1,0:T(8,128)(2,1)}), bf16[96,8,1280]{2,1,0:T(8,128)(2,1)S(1)}, u32[]{:S(2)}, u32[]{:S(2)}) async-start(bf16[96,8,1280]{2,1,0:T(8,128)(2,1)} %fusion.15), calls=%async_computation.7 | async-start | bytes 3932160 | tf_op jit(solution)/shard_map/all_to_all | solution.py:82
  595.6 6.8 copy-start.6
  595.6 6.8 copy-start.11
  595.7 6.8 copy-start.20
  595.7 6.8 copy-start.24
  602.4 3.2 copy-start.18
  602.4 3.2 copy-start.25
  760.0 4.2 copy-start.1
  (5 other events, 11.7 us)
Sparse Core Ops, SparseCore 0:
  53.3 61.8 all-reduce.6
  254.4 66.9 all-reduce.4
  323.6 71.8 all-gather.4
  525.5 51.0 all-gather.6
